TPU v7x, 32 devices: a whole 2x2x4 slice. The times are simulated.
32 devices in a mesh: grp: 2 (over x), exp: 4 (over z), tp: 4 (over y, core).
Axes of the slice: x: 2, y: 2, z: 4, core: 2. Of those that a mesh axis runs over, the one named last changes fastest.
Arguments:
- tokens: bfloat16 [256, 4096], P(('grp', 'exp'), 'tp'), may hold values from -6 to 6
- routes: int32 [256, 8], P(('grp', 'exp')), may hold values from 0 to 7, as said below
- gates: bfloat16 [256, 8], P(('grp', 'exp')), may hold values from 0.049804688 to 0.59765625
- w_gate: bfloat16 [8, 4096, 1536], P(('grp', 'exp'), None, 'tp'), may hold values from -0.09375 to 0.09375
- w_up: bfloat16 [8, 4096, 1536], P(('grp', 'exp'), None, 'tp'), may hold values from -0.09375 to 0.09375
- hidden_grad: bfloat16 [8, 256, 1536], P(('grp', 'exp'), None, 'tp'), may hold values from -6 to 6
Outputs:
- token_grad: bfloat16 [256, 4096], P(('grp', 'exp'), 'tp')
Inputs may be any that keep to these rules, and one draw needn't show every extreme that they name: `routes`: each row names 8 different experts, half of them in each of exactly two node groups (group g holds experts g * 4 to g * 4 + 3); all rows of one index of grp and exp share one of their two groups; among those rows no expert is named more than 32 times, and some expert is named exactly 32 times there.
All inputs are finite; a program needn't handle non-finite values.
Results may differ from a plain program's by a relative error of at most 0.012.
Values may be sent and summed in bfloat16 or wider, within the bound.
A program may use at most 64 MiB of HBM per device.

v0:
```python
import jax
import jax.numpy as jnp
from jax import lax
from jax.sharding import PartitionSpec as P


def local(tokens, routes, gates, w_gate, w_up, hidden_grad):
    group_count = lax.axis_size("grp")
    member_count = lax.axis_size("exp")
    experts = group_count * member_count
    tok_rows, part_width = tokens.shape
    per_token = routes.shape[1]
    slots = hidden_grad.shape[1]
    capacity = slots // experts
    flat_routes = routes.reshape(-1)
    onehot = (flat_routes[:, None] == jnp.arange(experts, dtype=jnp.int32)[None, :]).astype(
        jnp.int32
    )
    slot_ranks = jnp.sum((jnp.cumsum(onehot, axis=0) - onehot) * onehot, axis=1)
    blank_row = jnp.zeros((1, part_width), tokens.dtype)
    owner_row = jnp.arange(tok_rows * per_token, dtype=jnp.int32) // per_token
    slot_table = jnp.full((experts * capacity,), tok_rows, jnp.int32)
    slot_table = slot_table.at[flat_routes * capacity + slot_ranks].set(owner_row)
    outgoing = jnp.concatenate([tokens, blank_row], 0)[slot_table].reshape(
        group_count, member_count, capacity, part_width
    )
    across = lax.all_to_all(outgoing, "grp", split_axis=0, concat_axis=0, tiled=True)
    arrived = lax.all_to_all(across, "exp", split_axis=1, concat_axis=1, tiled=True)
    slot_rows = arrived.reshape(slots, part_width)
    weight_gate = w_gate[0]
    weight_up = w_up[0]
    piece = lax.all_gather(slot_rows, "tp", axis=1, tiled=True)
    pre_gate = jnp.dot(piece, weight_gate, preferred_element_type=jnp.float32)
    pre_up = jnp.dot(piece, weight_up, preferred_element_type=jnp.float32)
    sigmoid_gate = jax.nn.sigmoid(pre_gate)
    upstream = hidden_grad[0].astype(jnp.float32)
    grad_gate = (upstream * pre_up * sigmoid_gate * (1.0 + pre_gate * (1.0 - sigmoid_gate))).astype(
        jnp.bfloat16
    )
    grad_up = (upstream * pre_gate * sigmoid_gate).astype(jnp.bfloat16)
    contract = (((1,), (1,)), ((), ()))
    slot_term = lax.dot_general(
        grad_gate, weight_gate, contract, preferred_element_type=jnp.float32
    )
    slot_term = slot_term + lax.dot_general(
        grad_up, weight_up, contract, preferred_element_type=jnp.float32
    )
    summed = lax.psum_scatter(slot_term.astype(jnp.bfloat16), "tp", scatter_dimension=1, tiled=True)
    returned = lax.all_to_all(
        summed.reshape(group_count, member_count, capacity, part_width),
        "exp",
        split_axis=1,
        concat_axis=1,
        tiled=True,
    )
    at_owner = lax.all_to_all(returned, "grp", split_axis=0, concat_axis=0, tiled=True).reshape(
        experts * capacity, part_width
    )
    picked = at_owner[flat_routes * capacity + slot_ranks].reshape(tok_rows, per_token, part_width)
    combined = jnp.sum(gates.astype(jnp.float32)[:, :, None] * picked.astype(jnp.float32), axis=1)
    return combined.astype(jnp.bfloat16)


def solution(mesh):
    placed = (
        P(("grp", "exp"), "tp"),
        P(("grp", "exp"), None),
        P(("grp", "exp"), None),
        P(("grp", "exp"), None, "tp"),
        P(("grp", "exp"), None, "tp"),
        P(("grp", "exp"), None, "tp"),
    )
    return jax.shard_map(
        local, mesh=mesh, in_specs=placed, out_specs=P(("grp", "exp"), "tp"), check_vma=False
    )
```

profile of v0, /device:TPU:0, one launch (start us, length us, event | category | flops | bytes accessed | tf_op | source)
XLA Modules:
  0.0 159.1 jit_solution(16977373888070682862)
XLA Ops:
  6.5 0.9 copy.29
  7.6 0.7 broadcast_multiply_fusion
  8.3 0.6 reduce-window.6
  8.9 0.2 slice_reduce_fusion
  9.2 0.1 mul.45
  9.3 0.1 fusion.35
  9.4 1.4 scatter_custom_fusion
  10.9 0.8 concatenate.3
  11.7 2.0 %gather_fusion = bf16[256,1024]{1,0:T(8,128)(2,1)} fusion(bf16[33,1024]{1,0:T(8,128)(2,1)S(1)} %concatenate.3, s32[1024]{0:T(1024)S(1)} %pad_clamp_fusion.1), kind=kCustom, calls=%fused_computation | custom fusion | bytes 1049600 | tf_op jit(solution)/shard_map/gather | solution.py:24
  13.7 12.9 %all_to_all.20 = bf16[2,4,32,1024]{3,2,1,0:T(8,128)(2,1)S(1)} all-to-all(bf16[2,4,32,1024]{3,2,1,0:T(8,128)(2,1)} %bitcast.49), channel_id=1, replica_groups=mesh['grp'=2,'exp'=4,'tp'=4] {'grp'}, dimensions={0} | all-to-all | bytes 1048576 | tf_op jit(solution)/shard_map/all_to_all | solution.py:27
  26.6 18.5 %all_to_all.21 = bf16[2,4,32,1024]{3,2,0,1:T(8,128)(2,1)S(1)} all-to-all(bf16[2,4,32,1024]{3,2,0,1:T(8,128)(2,1)S(1)} %copy.31), channel_id=1, replica_groups=mesh['grp'=2,'exp'=4,'tp'=4] {'exp'}, dimensions={1} | all-to-all | bytes 1048576 | tf_op jit(solution)/shard_map/all_to_all | solution.py:28
  45.2 0.8 copy.32
  46.1 20.9 %all-gather.2.cloned.1.call-done = bf16[256,4096]{1,0:T(8,128)(2,1)} async-done(((bf16[256,1024]{1,0:T(8,128)(2,1)}), bf16[256,4096]{1,0:T(8,128)(2,1)}) %all-gather.2.cloned.1.call-update) | async-done | bytes 2097168 | tf_op jit(solution)/shard_map/all_gather | solution.py:32
  67.0 3.8 %fusion.3 = f32[256,384]{1,0:T(8,128)S(1)} fusion(bf16[256,4096]{1,0:T(8,128)(2,1)} %all-gather.2.cloned.1.call-done, bf16[1,4096,384]{2,1,0:T(8,128)(2,1)} %param.9), kind=kOutput, calls=%fused_computation.7 | convolution fusion | flops 805306368 | bytes 5636096 | tf_op jit(solution)/shard_map/dot_general | solution.py:33
  70.8 7.1 %fusion.1 = f32[256,4096]{1,0:T(8,128)} fusion(bf16[1,4096,384]{2,1,0:T(8,128)(2,1)} %param.9, bf16[256,4096]{1,0:T(8,128)(2,1)} %all-gather.2.cloned.1.call-done, bf16[1,4096,384]{2,1,0:T(8,128)(2,1)S(1)} %copy-done, f32[256,384]{1,0:T(8,128)S(1)} %fusion.3, bf16[1,256,384]{2,1,0:T(8,128)(2,1)} %param.11), kind=kOutput, calls=%fused_computation.5 | convolution fusion | flops 1611694080 | bytes 13172736 | tf_op jit(solution)/shard_map/dot_general | solution.py:42
  77.9 4.9 %fusion = bf16[256,4096]{1,0:T(8,128)(2,1)} fusion(f32[256,4096]{1,0:T(8,128)} %fusion.1, bf16[1,4096,384]{2,1,0:T(8,128)(2,1)S(1)} %copy-done, f32[256,384]{1,0:T(8,128)S(1)} %fusion.3, bf16[1,256,384]{2,1,0:T(8,128)(2,1)} %param.11), kind=kOutput, calls=%fused_computation.4 | convolution fusion | flops 808091648 | bytes 10027008 | tf_op jit(solution)/shard_map/dot_general | solution.py:45
  82.8 31.6 %reduce-scatter.2.cloned.1.call-done = bf16[256,1024]{1,0:T(8,128)(2,1)} async-done(((bf16[256,4096]{1,0:T(8,128)(2,1)}), bf16[256,1024]{1,0:T(8,128)(2,1)}) %reduce-scatter.2.cloned.1.call-update) | async-done | bytes 524304 | tf_op jit(solution)/shard_map/reduce_scatter | solution.py:48
  114.4 1.1 copy.33
  115.5 18.9 %all_to_all.22 = bf16[2,4,32,1024]{3,2,0,1:T(8,128)(2,1)S(1)} all-to-all(bf16[2,4,32,1024]{3,2,0,1:T(8,128)(2,1)S(1)} %copy.33), channel_id=1, replica_groups=mesh['grp'=2,'exp'=4,'tp'=4] {'exp'}, dimensions={1} | all-to-all | bytes 1048576 | tf_op jit(solution)/shard_map/all_to_all | solution.py:49
  134.4 0.9 copy.34
  135.3 4.2 %all-to-all-start.3 = ((bf16[2,4,32,1024]{3,2,1,0:T(8,128)(2,1)}), bf16[2,4,32,1024]{3,2,1,0:T(8,128)(2,1)}, u32[]{:S(2)}, u32[]{:S(2)}) async-start(bf16[2,4,32,1024]{3,2,1,0:T(8,128)(2,1)} %copy.34), calls=%async_computation.4 | async-start | bytes 1048576 | tf_op jit(solution)/shard_map/all_to_all | solution.py:56
  139.6 7.1 %all-to-all-done.3 = bf16[2,4,32,1024]{3,2,1,0:T(8,128)(2,1)} async-done(((bf16[2,4,32,1024]{3,2,1,0:T(8,128)(2,1)}), bf16[2,4,32,1024]{3,2,1,0:T(8,128)(2,1)}, u32[]{:S(2)}, u32[]{:S(2)}) %all-to-all-start.3) | async-done | bytes 524320 | tf_op jit(solution)/shard_map/all_to_all | solution.py:56
  146.7 3.5 %gather_fusion.1 = bf16[256,1024]{1,0:T(8,128)(2,1)} fusion(bf16[256,1024]{1,0:T(8,128)(2,1)} %bitcast.11, s32[1024]{0:T(1024)S(1)} %pad_clamp_fusion), kind=kCustom, calls=%fused_computation.1 | custom fusion | bytes 1049600 | tf_op jit(solution)/shard_map/gather | solution.py:59
  150.2 2.1 %fusion.22 = bf16[32,1024]{1,0:T(8,128)(2,1)} fusion(bf16[256,1024]{1,0:T(8,128)(2,1)} %gather_fusion.1, f32[32,8]{1,0:T(8,128)S(1)} %copy.27), kind=kLoop, calls=%fused_computation.17 | loop fusion | flops 753664 | bytes 590848 | tf_op jit(solution)/shard_map/reduce_sum | solution.py:60
  (21 shorter events, 0.5 us)
Async XLA Ops:
  6.5 64.3 %copy-start = (bf16[1,4096,384]{2,1,0:T(8,128)(2,1)S(1)}, bf16[1,4096,384]{2,1,0:T(8,128)(2,1)}, u32[]{:S(2)}) copy-start(bf16[1,4096,384]{2,1,0:T(8,128)(2,1)} %param.10) | copy-start | bytes 9437188
  6.5 60.5 %all-gather.2.cloned.1.call-start = ((), (), s32[]{:S(2)}) async-start(), calls=%async_computation.5 | async-start | bytes 2621440 | tf_op jit(solution)/shard_map/all_gather | solution.py:32
  46.0 68.4 %reduce-scatter.2.cloned.1.call-start = ((), (), s32[]{:S(2)}) async-start(), calls=%async_computation.6 | async-start | bytes 2621440 | tf_op jit(solution)/shard_map/reduce_scatter | solution.py:48
  82.8 56.7 %copy-start.1 = (bf16[32,8]{0,1:T(8,128)(2,1)S(1)}, bf16[32,8]{0,1:T(8,128)(2,1)}, u32[]{:S(2)}) copy-start(bf16[32,8]{0,1:T(8,128)(2,1)} %param.8) | copy-start | bytes 1540
  135.3 11.4 %all-to-all-start.3 = ((bf16[2,4,32,1024]{3,2,1,0:T(8,128)(2,1)}), bf16[2,4,32,1024]{3,2,1,0:T(8,128)(2,1)}, u32[]{:S(2)}, u32[]{:S(2)}) async-start(bf16[2,4,32,1024]{3,2,1,0:T(8,128)(2,1)} %copy.34), calls=%async_computation.4 | async-start | bytes 1048576 | tf_op jit(solution)/shard_map/all_to_all | solution.py:56
Sparse Core Ops, SparseCore 0:
  46.2 20.8 all-gather.1
  82.9 31.4 reduce-scatter.1
where the time goes:
time: 160 us; the launch traced here: 159 us
  waiting for transfers between devices  59.6 us (37%)
  blocking collectives  50.4 us (32%)
  matrix products  15.8 us (10%)
  between operations  13.5 us (8%)
  local copies, waits for them, and re-layouts  12.1 us (8%)
  starting transfers between devices  4.24 us (3%)
  other arithmetic  3.49 us (2%)
    reduce_scatter x1, waiting for transfers between devices, local(): lax.psum_scatter(slot_term.astype(jnp.bfloat16), 'tp', scatter_dimension=...  31.6 us
    all_gather x1, waiting for transfers between devices, local(): piece = lax.all_gather(slot_rows, 'tp', axis=1, tiled=True)  20.9 us
    all_to_all x1, blocking collectives, local(): lax.all_to_all(summed.reshape(group_count, member_count, capacity, part_w...  18.9 us
    all_to_all x1, blocking collectives, local(): lax.all_to_all(across, 'exp', split_axis=1, concat_axis=1, tiled=True)  18.5 us
    all_to_all x1, blocking collectives, local(): lax.all_to_all(outgoing, 'grp', split_axis=0, concat_axis=0, tiled=True)  12.9 us
    all_to_all x1, waiting for transfers between devices, local(): lax.all_to_all(returned, 'grp', split_axis=0, concat_axis=0, tiled=True)  7.11 us
    dot_general x1, matrix products, local(): lax.dot_general(grad_gate, weight_gate, contract, preferred_element_type=...  7.06 us
    dot_general x1, matrix products, local(): lax.dot_general(grad_up, weight_up, contract, preferred_element_type=jnp....  4.93 us
  transfers between devices with their start and end apart: 3, of which 3 were waited for; matrix products, arithmetic and copies ran while one was open for 0% of the time, Pallas kernels for 0%

commit v1 on v0

--- a/solution.py
+++ b/solution.py
@@ -1,10 +1,16 @@
+import functools
+
 import jax
 import jax.numpy as jnp
 from jax import lax
+from jax.experimental import pallas as pl
+from jax.experimental.pallas import tpu as pltpu
 from jax.sharding import PartitionSpec as P
 
-
-def local(tokens, routes, gates, w_gate, w_up, hidden_grad):
+MESH = pl.DeviceIdType.MESH
+
+
+def routed(tokens, routes, gates, w_gate, w_up, hidden_grad):
     group_count = lax.axis_size("grp")
     member_count = lax.axis_size("exp")
     experts = group_count * member_count
@@ -61,6 +67,278 @@
     return combined.astype(jnp.bfloat16)
 
 
+def dense_kernel(
+    tok_hbm, routes_hbm, gates_hbm, wg_hbm, wu_hbm, hid_hbm, out_ref,
+    rt, gt, hid, w, x, gate_all, pre, grads, p_sib, r_sib, p_own, stage, recv, c_send, c_recv,
+    local_sem, send_sem, recv_sem,
+):
+    n_exp = 4
+    rows, width = tok_hbm.shape
+    half = width // 2
+    group = n_exp * rows
+    ht = hid.shape[1]
+    gx, ez, tp = lax.axis_index("grp"), lax.axis_index("exp"), lax.axis_index("tp")
+    core = lax.rem(tp, 2)
+    ty = tp // 2
+    ox, oy, oc = 1 - gx, 1 - ty, 1 - core
+    zk = [ez, ez + 1 - 2 * lax.rem(ez, 2), lax.rem(ez + 2, n_exp), n_exp - 1 - ez]
+    q = 2 * ty + core
+    qy = 2 * oy + core
+    qc = 2 * ty + oc
+    qcy = 2 * oy + oc
+    to_x, to_y, to_c = (ox, ez, tp), (gx, ez, qy), (gx, ez, qc)
+    to_z = [None] + [(gx, zk[k], tp) for k in (1, 2, 3)]
+
+    def row(gr, z):
+        return pl.multiple_of((gr * n_exp + z) * rows, rows)
+
+    counter = [0]
+    sent = []
+
+    def remote(src, dst, device):
+        i = counter[0]
+        counter[0] += 1
+        c = pltpu.make_async_remote_copy(
+            src_ref=src, dst_ref=dst, send_sem=send_sem.at[i], recv_sem=recv_sem.at[i],
+            device_id=device, device_id_type=MESH,
+        )
+        c.start()
+        sent.append(c)
+        return c
+
+    mine = pl.ds(row(gx, ez), rows)
+    loc = [
+        pltpu.make_async_copy(tok_hbm.at[:, pl.ds(0, half)], x.at[2 * q, mine, :], local_sem.at[0]),
+        pltpu.make_async_copy(tok_hbm.at[:, pl.ds(half, half)], x.at[2 * q + 1, mine, :], local_sem.at[1]),
+        pltpu.make_async_copy(routes_hbm, rt, local_sem.at[2]),
+        pltpu.make_async_copy(gates_hbm, gt, local_sem.at[3]),
+        pltpu.make_async_copy(wg_hbm, w.at[:, :, pl.ds(0, ht)], local_sem.at[4]),
+        pltpu.make_async_copy(wu_hbm, w.at[:, :, pl.ds(ht, ht)], local_sem.at[5]),
+        pltpu.make_async_copy(hid_hbm, hid, local_sem.at[6]),
+    ]
+    for c in loc:
+        c.start()
+    barrier = pltpu.get_barrier_semaphore()
+    partners = [to_x, to_y, to_c] + to_z[1:]
+    for d in partners:
+        pl.semaphore_signal(barrier, inc=1, device_id=d, device_id_type=MESH)
+    loc[0].wait()
+    loc[1].wait()
+    pl.semaphore_wait(barrier, len(partners))
+
+    def block(quarter, gr, z):
+        return x.at[pl.ds(2 * quarter, 2), pl.ds(row(gr, z), rows), :]
+
+    def piece(quarter, h, gr, z):
+        return x.at[2 * quarter + h, pl.ds(row(gr, z), rows), :]
+
+    def same(ref, device):
+        return remote(ref, ref, device)
+
+    zc, xc, yc, fa, fb = [None] * 4, [None] * 4, [None] * 4, [None] * 4, [None] * 4
+    core_copies = [[None] * 4 for _ in range(4)]
+    for k in (3, 2, 1):
+        zc[k] = same(block(q, gx, ez), to_z[k])
+
+    def column(k):
+        if k:
+            zc[k].wait_recv()
+        xc[k] = same(block(q, gx, zk[k]), to_x)
+        yc[k] = same(block(q, gx, zk[k]), to_y)
+        core_copies[0][k] = same(block(q, gx, zk[k]), to_c)
+
+    def onward(k):
+        xc[k].wait_recv()
+        fa[k] = same(piece(q, 0, ox, zk[k]), to_y)
+        core_copies[1][k] = same(block(q, ox, zk[k]), to_c)
+        yc[k].wait_recv()
+        fb[k] = same(piece(qy, 1, gx, zk[k]), to_x)
+        core_copies[2][k] = same(block(qy, gx, zk[k]), to_c)
+
+    column(0)
+    loc[2].wait()
+    loc[3].wait()
+    lanes = lax.broadcasted_iota(jnp.int32, (rows, 128), 1)
+    table = jnp.zeros((rows, 128), jnp.float32)
+    chosen = rt[...]
+    values = gt[...].astype(jnp.float32)
+    for k in range(chosen.shape[1]):
+        table = table + jnp.where(lanes == chosen[:, k : k + 1], values[:, k : k + 1], 0.0)
+    gate_all[mine, :] = table.astype(jnp.bfloat16)
+    own_gates = gate_all.at[mine, :]
+    gz = [same(own_gates, to_z[k]) for k in (1, 2, 3)]
+    column(1)
+    onward(0)
+    column(2)
+    onward(1)
+    column(3)
+    for c in gz:
+        c.wait_recv()
+    gate_column = gate_all.at[pl.ds(row(gx, 0), group), :]
+    gcol = same(gate_column, to_x)
+    onward(2)
+    onward(3)
+    for c in loc[4:]:
+        c.wait()
+
+    def first(quarter):
+        return jnp.dot(
+            x[2 * quarter], w[2 * quarter], preferred_element_type=jnp.float32
+        ) + jnp.dot(x[2 * quarter + 1], w[2 * quarter + 1], preferred_element_type=jnp.float32)
+
+    pre[...] = first(q)
+    for k in range(4):
+        fa[k].wait_recv()
+        fb[k].wait_recv()
+        core_copies[3][k] = same(block(qy, ox, zk[k]), to_c)
+    pre[...] += first(qy)
+    for k in range(4):
+        core_copies[0][k].wait_recv()
+        core_copies[1][k].wait_recv()
+    pre[...] += first(qc)
+    gcol.wait_recv()
+    expert = gx * n_exp + ez
+    total_rows = pre.shape[0]
+    lane = lax.broadcasted_iota(jnp.int32, (total_rows, 128), 1)
+    scale = jnp.sum(
+        jnp.where(lane == expert, gate_all[...].astype(jnp.float32), 0.0), axis=1, keepdims=True
+    )
+    for k in range(4):
+        core_copies[2][k].wait_recv()
+        core_copies[3][k].wait_recv()
+    both = pre[...] + first(qcy)
+    pre_gate, pre_up = both[:, :ht], both[:, ht:]
+    sg = jax.nn.sigmoid(pre_gate)
+    up = hid[...].astype(jnp.float32) * scale * sg
+    grads[:, :ht] = (up * pre_up * (1.0 + pre_gate * (1.0 - sg))).astype(jnp.bfloat16)
+    grads[:, ht:] = (up * pre_gate).astype(jnp.bfloat16)
+
+    def second(part):
+        return lax.dot_general(
+            grads[...], w[part], (((1,), (1,)), ((), ())), preferred_element_type=jnp.float32
+        )
+
+    sib = []
+    for j in range(4):
+        p_sib[j] = second(2 * (qcy if j < 2 else qc) + j % 2).astype(jnp.bfloat16)
+        sib.append(remote(p_sib.at[j], r_sib.at[j], to_c))
+    for j in range(4):
+        p_own[j] = second(2 * (qy if j < 2 else q) + j % 2)
+    pair = 2 * rows
+    far = 1 - ez // 2
+    offs = [pl.multiple_of(far * pair, pair), pl.multiple_of((1 - far) * pair, pair)]
+
+    def at(gr, o):
+        return pl.ds(pl.multiple_of(gr * group + offs[o], pair), pair)
+
+    da, db, sx, sy = {}, {}, {}, {}
+
+    def own(j, gr, o):
+        return p_own[j, at(gr, o), :] + r_sib[j, at(gr, o), :].astype(jnp.float32)
+
+    def send(slot, value, o, device):
+        stage[slot, o] = value.astype(jnp.bfloat16)
+        return remote(stage.at[slot, o], recv.at[slot, o], device)
+
+    sib[0].wait_recv()
+    for o in range(2):
+        da[o] = send(0, own(0, ox, o), o, to_y)
+    sib[1].wait_recv()
+    for o in range(2):
+        db[o] = send(1, own(1, ox, o), o, to_x)
+    for o in range(2):
+        sy[o, 0] = send(2, own(0, gx, o), o, to_y)
+    sib[3].wait_recv()
+    for o in range(2):
+        sx[o, 1] = send(3, own(3, ox, o), o, to_x)
+    sib[2].wait_recv()
+    for o in range(2):
+        da[o].wait_recv()
+        sx[o, 0] = send(4, own(2, ox, o) + recv[0, o].astype(jnp.float32), o, to_x)
+        db[o].wait_recv()
+        sy[o, 1] = send(5, own(1, gx, o) + recv[1, o].astype(jnp.float32), o, to_y)
+    back = {}
+    for o in range(2):
+        sy[o, 0].wait_recv()
+        sx[o, 1].wait_recv()
+        sx[o, 0].wait_recv()
+        sy[o, 1].wait_recv()
+        for k in ((2, 3) if o == 0 else (1, 0)):
+            r = pl.multiple_of(lax.rem(zk[k], 2) * rows, rows)
+            s = pl.ds(r, rows)
+            here = pl.ds(pl.multiple_of(gx * group + zk[k] * rows, rows), rows)
+            for h, slots in ((0, (4, 2)), (1, (3, 5))):
+                v = p_own[2 + h, here, :] + r_sib[2 + h, here, :].astype(jnp.float32)
+                for slot in slots:
+                    v = v + recv[slot, o, s, :].astype(jnp.float32)
+                if k:
+                    c_send[k - 1, h] = v.astype(jnp.bfloat16)
+                else:
+                    p_own[2 + h, here, :] = v
+            if k:
+                back[k] = remote(c_send.at[k - 1], c_recv.at[k - 1], to_z[k])
+    here = pl.ds(row(gx, ez), rows)
+    for k in (1, 2, 3):
+        back[k].wait_recv()
+    for h in range(2):
+        v = p_own[2 + h, here, :]
+        for k in range(3):
+            v = v + c_recv[k, h].astype(jnp.float32)
+        out_ref[:, h * half : (h + 1) * half] = v.astype(jnp.bfloat16)
+    for c in sent:
+        c.wait_send()
+
+
+def dense(tokens, routes, gates, w_gate, w_up, hidden_grad):
+    rows, width = tokens.shape
+    half = width // 2
+    _, depth, ht = w_gate.shape
+    slots = hidden_grad.shape[1]
+    parts = depth // half
+    bf16, f32 = jnp.bfloat16, jnp.float32
+    any_space = pl.BlockSpec(memory_space=pl.ANY)
+    n_copies = 3 + 8 + 8 + 16 + 4 + 4 + 12 + 3
+    return pl.pallas_call(
+        dense_kernel,
+        out_shape=jax.ShapeDtypeStruct((rows, width), bf16),
+        in_specs=[any_space] * 6,
+        out_specs=pl.BlockSpec(memory_space=pltpu.VMEM),
+        scratch_shapes=[
+            pltpu.VMEM(routes.shape, jnp.int32),
+            pltpu.VMEM(gates.shape, bf16),
+            pltpu.VMEM((slots, ht), bf16),
+            pltpu.VMEM((parts, half, 2 * ht), bf16),
+            pltpu.VMEM((parts, slots, half), bf16),
+            pltpu.VMEM((slots, 128), bf16),
+            pltpu.VMEM((slots, 2 * ht), f32),
+            pltpu.VMEM((slots, 2 * ht), bf16),
+            pltpu.VMEM((4, slots, half), bf16),
+            pltpu.VMEM((4, slots, half), bf16),
+            pltpu.VMEM((4, slots, half), f32),
+            pltpu.VMEM((6, 2, 2 * rows, half), bf16),
+            pltpu.VMEM((6, 2, 2 * rows, half), bf16),
+            pltpu.VMEM((3, 2, rows, half), bf16),
+            pltpu.VMEM((3, 2, rows, half), bf16),
+            pltpu.SemaphoreType.DMA((7,)),
+            pltpu.SemaphoreType.DMA((n_copies,)),
+            pltpu.SemaphoreType.DMA((n_copies,)),
+        ],
+        compiler_params=pltpu.CompilerParams(
+            collective_id=0, has_side_effects=True, vmem_limit_bytes=56 << 20
+        ),
+        cost_estimate=pl.CostEstimate(
+            flops=8 * slots * depth * ht, bytes_accessed=4 * depth * ht, transcendentals=slots * ht
+        ),
+    )(
+        tokens,
+        routes,
+        gates,
+        w_gate.reshape(parts, half, ht),
+        w_up.reshape(parts, half, ht),
+        hidden_grad.reshape(slots, ht),
+    )
+
+
 def solution(mesh):
     placed = (
         P(("grp", "exp"), "tp"),
@@ -70,6 +348,14 @@
         P(("grp", "exp"), None, "tp"),
         P(("grp", "exp"), None, "tp"),
     )
+    sizes = (mesh.shape["grp"], mesh.shape["exp"], mesh.shape["tp"])
+    experts = sizes[0] * sizes[1]
+
+    def local(tokens, routes, *rest):
+        if sizes == (2, 4, 4) and routes.shape[1] == experts:
+            return dense(tokens, routes, *rest)
+        return routed(tokens, routes, *rest)
+
     return jax.shard_map(
         local, mesh=mesh, in_specs=placed, out_specs=P(("grp", "exp"), "tp"), check_vma=False
     )

time: 160 us -> 48.2 us (0.30)
  waiting for transfers between devices: 59.6 us -> 0 us
  blocking collectives: 50.4 us -> 0 us
  Pallas kernels: 0 us -> 43.8 us
  matrix products: 15.8 us -> 0 us
  between operations: 13.5 us -> 0.01 us
  local copies, waits for them, and re-layouts: 12.1 us -> 4.19 us
  starting transfers between devices: 4.24 us -> 0 us
  other arithmetic: 3.49 us -> 0 us
    all_to_all x3 -> x0, blocking collectives: 50.4 us -> none  [the longest x1 18.9 us: local(): lax.all_to_all(summed.reshape(group_count, member_count, capacity, part_w...]
    pallas_call x0 -> x1, Pallas kernels: none -> 43.8 us  [dense(): pl.pallas_call(dense_kernel, out_shape=jax.ShapeDtypeStruct((rows, width)...]
    reduce_scatter x1 -> x0, waiting for transfers between devices: 31.6 us -> none  [local(): lax.psum_scatter(slot_term.astype(jnp.bfloat16), 'tp', scatter_dimension=...]
    all_gather x1 -> x0, waiting for transfers between devices: 20.9 us -> none  [local(): piece = lax.all_gather(slot_rows, 'tp', axis=1, tiled=True)]
    dot_general x3 -> x0, matrix products: 15.8 us -> none  [the longest x1 7.06 us: local(): lax.dot_general(grad_gate, weight_gate, contract, preferred_element_type=...]
    all_to_all x1 -> x0, waiting for transfers between devices: 7.11 us -> none  [local(): lax.all_to_all(returned, 'grp', split_axis=0, concat_axis=0, tiled=True)]
    gather x2 -> x0, local copies, waits for them, and re-layouts: 5.43 us -> none  [the longest x1 3.48 us: local(): at_owner[flat_routes * capacity + slot_ranks]]
    all_to_all x1 -> x0, starting transfers between devices: 4.2 us -> none  [local(): lax.all_to_all(returned, 'grp', split_axis=0, concat_axis=0, tiled=True)]
  transfers between devices with their start and end apart: 3 -> 0, of which waited for: 3 -> 0; matrix products, arithmetic and copies ran while one was open for 0% -> 0% of each run, Pallas kernels for 0% -> 0%
where the time goes in v1:
time: 48.2 us; the launch traced here: 48 us
  Pallas kernels  43.8 us (91%)
  local copies, waits for them, and re-layouts  4.19 us (9%)
    pallas_call x1, Pallas kernels, dense(): pl.pallas_call(dense_kernel, out_shape=jax.ShapeDtypeStruct((rows, width)...  43.8 us
    unnamed x3, local copies, waits for them, and re-layouts  4.19 us

profile of v1, /device:TPU:0, one launch (start us, length us, event | category | flops | bytes accessed | tf_op | source)
XLA Modules:
  0.0 48.0 jit_solution(14424125463776299577)
XLA Ops:
  0.0 1.3 %copy.8.gates_hbm = bf16[32,8]{1,0:T(8,128)(2,1)} copy(bf16[32,8]{0,1:T(8,128)(2,1)} %param.8) | data formatting | bytes 1024 | tf_op args[2]
  1.4 1.4 %copy.7.routes_hbm = s32[32,8]{1,0:T(8,128)} copy(s32[32,8]{0,1:T(8,128)} %param.7) | data formatting | bytes 2048 | tf_op args[1]
  2.7 43.8 %shard_map.64 = bf16[32,1024]{1,0:T(8,128)(2,1)} custom-call(bf16[32,1024]{1,0:T(8,128)(2,1)} %tok_hbm.1, s32[32,8]{1,0:T(8,128)} %copy.7.routes_hbm, bf16[32,8]{1,0:T(8,128)(2,1)} %copy.8.gates_hbm, bf16[8,512,384]{2,1,0:T(8,128)(2,1)} %bitcast.3, bf16[8,512,384]{2,1,0:T(8,128)(2,1)} %bitcast.4, bf16[256,384]{1,0:T(8,128)(2,1)} %bitcast.5), custom_call_target="tpu_custom_call" | custom-call | flops 3221225472 | bytes 6291456 | tf_op jit(solution)/shard_map/pallas_call | solution.py:301
  46.5 1.5 %copy.10 = bf16[32,1024]{1,0:T(8,128)(2,1)} copy(bf16[32,1024]{1,0:T(8,128)(2,1)} %shard_map.64) | data formatting | bytes 131072

commit v2 on v1

--- a/solution.py
+++ b/solution.py
@@ -87,7 +87,7 @@
     qc = 2 * ty + oc
     qcy = 2 * oy + oc
     to_x, to_y, to_c = (ox, ez, tp), (gx, ez, qy), (gx, ez, qc)
-    to_z = [None] + [(gx, zk[k], tp) for k in (1, 2, 3)]
+    to_z = [(gx, z, tp) for z in zk]
 
     def row(gr, z):
         return pl.multiple_of((gr * n_exp + z) * rows, rows)
@@ -116,7 +116,7 @@
         pltpu.make_async_copy(wu_hbm, w.at[:, :, pl.ds(ht, ht)], local_sem.at[5]),
         pltpu.make_async_copy(hid_hbm, hid, local_sem.at[6]),
     ]
-    for c in loc:
+    for c in loc[:4]:
         c.start()
     barrier = pltpu.get_barrier_semaphore()
     partners = [to_x, to_y, to_c] + to_z[1:]
@@ -135,10 +135,9 @@
     def same(ref, device):
         return remote(ref, ref, device)
 
-    zc, xc, yc, fa, fb = [None] * 4, [None] * 4, [None] * 4, [None] * 4, [None] * 4
+    xc, yc, fa, fb = [None] * 4, [None] * 4, [None] * 4, [None] * 4
     core_copies = [[None] * 4 for _ in range(4)]
-    for k in (3, 2, 1):
-        zc[k] = same(block(q, gx, ez), to_z[k])
+    zc = [None] + [same(block(q, gx, ez), to_z[k]) for k in (1, 2, 3)]
 
     def column(k):
         if k:
@@ -156,14 +155,23 @@
         core_copies[2][k] = same(block(qy, gx, zk[k]), to_c)
 
     column(0)
+    for c in loc[4:]:
+        c.start()
     loc[2].wait()
     loc[3].wait()
-    lanes = lax.broadcasted_iota(jnp.int32, (rows, 128), 1)
+    lanes = lax.broadcasted_iota(jnp.int32, (rows, 128), 1).astype(jnp.float32)
     table = jnp.zeros((rows, 128), jnp.float32)
-    chosen = rt[...]
-    values = gt[...].astype(jnp.float32)
-    for k in range(chosen.shape[1]):
-        table = table + jnp.where(lanes == chosen[:, k : k + 1], values[:, k : k + 1], 0.0)
+    chosen = rt[...].astype(jnp.float32)
+    values = gt[...]
+    shape = (rows, rows)
+    eye = lax.broadcasted_iota(jnp.int32, shape, 0) == lax.broadcasted_iota(jnp.int32, shape, 1)
+
+    def upright(line):
+        return jnp.sum(jnp.where(eye, line, 0.0), axis=1, keepdims=True)
+
+    for k in range(chosen.shape[0]):
+        pick = lanes == upright(chosen[k : k + 1, :])
+        table = table + jnp.where(pick, upright(values[k : k + 1, :]), 0.0)
     gate_all[mine, :] = table.astype(jnp.bfloat16)
     own_gates = gate_all.at[mine, :]
     gz = [same(own_gates, to_z[k]) for k in (1, 2, 3)]
@@ -224,64 +232,69 @@
         sib.append(remote(p_sib.at[j], r_sib.at[j], to_c))
     for j in range(4):
         p_own[j] = second(2 * (qy if j < 2 else q) + j % 2)
-    pair = 2 * rows
-    far = 1 - ez // 2
-    offs = [pl.multiple_of(far * pair, pair), pl.multiple_of((1 - far) * pair, pair)]
-
-    def at(gr, o):
-        return pl.ds(pl.multiple_of(gr * group + offs[o], pair), pair)
-
     da, db, sx, sy = {}, {}, {}, {}
 
-    def own(j, gr, o):
-        return p_own[j, at(gr, o), :] + r_sib[j, at(gr, o), :].astype(jnp.float32)
-
-    def send(slot, value, o, device):
-        stage[slot, o] = value.astype(jnp.bfloat16)
-        return remote(stage.at[slot, o], recv.at[slot, o], device)
+    def own(j, gr, k):
+        at = pl.ds(row(gr, zk[k]), rows)
+        return p_own[j, at, :] + r_sib[j, at, :].astype(jnp.float32)
+
+    def got(slot, k):
+        return recv[slot, k].astype(jnp.float32)
+
+    def send(slot, value, k, device):
+        stage[slot, k] = value.astype(jnp.bfloat16)
+        return remote(stage.at[slot, k], recv.at[slot, k], device)
+
+    def diagonal(k):
+        da[k] = send(0, own(0, ox, k), k, to_y)
+        db[k] = send(1, own(1, ox, k), k, to_x)
+
+    def plain(k):
+        sy[0, k] = send(2, own(0, gx, k), k, to_y)
+        sx[1, k] = send(3, own(3, ox, k), k, to_x)
+
+    def joined(k):
+        da[k].wait_recv()
+        sx[0, k] = send(4, own(2, ox, k) + got(0, k), k, to_x)
+        db[k].wait_recv()
+        sy[1, k] = send(5, own(1, gx, k) + got(1, k), k, to_y)
+
+    back, mine_sum = {}, [None, None]
+
+    def finish(k):
+        for c in (sy[0, k], sx[1, k], sx[0, k], sy[1, k]):
+            c.wait_recv()
+        for h, slots in ((0, (4, 2)), (1, (3, 5))):
+            v = own(2 + h, gx, k) + got(slots[0], k) + got(slots[1], k)
+            if k:
+                c_send[k - 1, h] = v.astype(jnp.bfloat16)
+            else:
+                mine_sum[h] = v
+        if k:
+            back[k] = remote(c_send.at[k - 1], c_recv.at[k - 1], to_z[k])
 
     sib[0].wait_recv()
-    for o in range(2):
-        da[o] = send(0, own(0, ox, o), o, to_y)
     sib[1].wait_recv()
-    for o in range(2):
-        db[o] = send(1, own(1, ox, o), o, to_x)
-    for o in range(2):
-        sy[o, 0] = send(2, own(0, gx, o), o, to_y)
+    diagonal(2)
+    diagonal(3)
+    sib[2].wait_recv()
     sib[3].wait_recv()
-    for o in range(2):
-        sx[o, 1] = send(3, own(3, ox, o), o, to_x)
-    sib[2].wait_recv()
-    for o in range(2):
-        da[o].wait_recv()
-        sx[o, 0] = send(4, own(2, ox, o) + recv[0, o].astype(jnp.float32), o, to_x)
-        db[o].wait_recv()
-        sy[o, 1] = send(5, own(1, gx, o) + recv[1, o].astype(jnp.float32), o, to_y)
-    back = {}
-    for o in range(2):
-        sy[o, 0].wait_recv()
-        sx[o, 1].wait_recv()
-        sx[o, 0].wait_recv()
-        sy[o, 1].wait_recv()
-        for k in ((2, 3) if o == 0 else (1, 0)):
-            r = pl.multiple_of(lax.rem(zk[k], 2) * rows, rows)
-            s = pl.ds(r, rows)
-            here = pl.ds(pl.multiple_of(gx * group + zk[k] * rows, rows), rows)
-            for h, slots in ((0, (4, 2)), (1, (3, 5))):
-                v = p_own[2 + h, here, :] + r_sib[2 + h, here, :].astype(jnp.float32)
-                for slot in slots:
-                    v = v + recv[slot, o, s, :].astype(jnp.float32)
-                if k:
-                    c_send[k - 1, h] = v.astype(jnp.bfloat16)
-                else:
-                    p_own[2 + h, here, :] = v
-            if k:
-                back[k] = remote(c_send.at[k - 1], c_recv.at[k - 1], to_z[k])
-    here = pl.ds(row(gx, ez), rows)
+    plain(2)
+    plain(3)
+    diagonal(1)
+    diagonal(0)
+    joined(2)
+    joined(3)
+    plain(1)
+    plain(0)
+    joined(1)
+    joined(0)
+    for k in (2, 3, 1, 0):
+        finish(k)
     for k in (1, 2, 3):
         back[k].wait_recv()
     for h in range(2):
-        v = p_own[2 + h, here, :]
+        v = mine_sum[h]
         for k in range(3):
             v = v + c_recv[k, h].astype(jnp.float32)
         out_ref[:, h * half : (h + 1) * half] = v.astype(jnp.bfloat16)
@@ -297,15 +310,15 @@
     parts = depth // half
     bf16, f32 = jnp.bfloat16, jnp.float32
     any_space = pl.BlockSpec(memory_space=pl.ANY)
-    n_copies = 3 + 8 + 8 + 16 + 4 + 4 + 12 + 3
+    n_copies = 3 + 8 + 8 + 16 + 4 + 4 + 24 + 3
     return pl.pallas_call(
         dense_kernel,
         out_shape=jax.ShapeDtypeStruct((rows, width), bf16),
         in_specs=[any_space] * 6,
         out_specs=pl.BlockSpec(memory_space=pltpu.VMEM),
         scratch_shapes=[
-            pltpu.VMEM(routes.shape, jnp.int32),
-            pltpu.VMEM(gates.shape, bf16),
+            pltpu.VMEM(routes.shape[::-1], jnp.int32),
+            pltpu.VMEM(gates.shape[::-1], f32),
             pltpu.VMEM((slots, ht), bf16),
             pltpu.VMEM((parts, half, 2 * ht), bf16),
             pltpu.VMEM((parts, slots, half), bf16),
@@ -315,8 +328,8 @@
             pltpu.VMEM((4, slots, half), bf16),
             pltpu.VMEM((4, slots, half), bf16),
             pltpu.VMEM((4, slots, half), f32),
-            pltpu.VMEM((6, 2, 2 * rows, half), bf16),
-            pltpu.VMEM((6, 2, 2 * rows, half), bf16),
+            pltpu.VMEM((6, 4, rows, half), bf16),
+            pltpu.VMEM((6, 4, rows, half), bf16),
             pltpu.VMEM((3, 2, rows, half), bf16),
             pltpu.VMEM((3, 2, rows, half), bf16),
             pltpu.SemaphoreType.DMA((7,)),
@@ -331,8 +344,8 @@
         ),
     )(
         tokens,
-        routes,
-        gates,
+        routes.T,
+        gates.T.astype(f32),
         w_gate.reshape(parts, half, ht),
         w_up.reshape(parts, half, ht),
         hidden_grad.reshape(slots, ht),

time: 48.2 us -> 44 us (0.913)
  Pallas kernels: 43.8 us -> 41 us
  local copies, waits for them, and re-layouts: 4.19 us -> 1.47 us
  other arithmetic: 0 us -> 1.27 us
    pallas_call x1, Pallas kernels: 43.8 us -> 41 us  [dense(): pl.pallas_call(dense_kernel, out_shape=jax.ShapeDtypeStruct((rows, width)...]
    unnamed x3 -> x1, local copies, waits for them, and re-layouts: 4.19 us -> 1.47 us
    convert_element_type x0 -> x1, other arithmetic: none -> 1.27 us  [dense(): gates.T.astype(f32)]
where the time goes in v2:
time: 44 us; the launch traced here: 43.8 us
  Pallas kernels  41 us (93%)
  local copies, waits for them, and re-layouts  1.47 us (3%)
  other arithmetic  1.27 us (3%)
    pallas_call x1, Pallas kernels, dense(): pl.pallas_call(dense_kernel, out_shape=jax.ShapeDtypeStruct((rows, width)...  41 us
    unnamed x1, local copies, waits for them, and re-layouts  1.47 us
    convert_element_type x1, other arithmetic, dense(): gates.T.astype(f32)  1.27 us

profile of v2, /device:TPU:0, one launch (start us, length us, event | category | flops | bytes accessed | tf_op | source)
XLA Modules:
  0.0 43.8 jit_solution(14226455386157907510)
XLA Ops:
  0.0 1.3 %convert_bitcast_fusion.gates_hbm = f32[8,32]{1,0:T(8,128)} fusion(bf16[32,8]{0,1:T(8,128)(2,1)} %param.8), kind=kLoop, calls=%fused_computation | loop fusion | flops 256 | bytes 1536 | tf_op jit(solution)/shard_map/convert_element_type | solution.py:348
  1.3 41.0 %shard_map.64 = bf16[32,1024]{1,0:T(8,128)(2,1)} custom-call(bf16[32,1024]{1,0:T(8,128)(2,1)} %tok_hbm.1, s32[8,32]{1,0:T(8,128)} %bitcast.9, f32[8,32]{1,0:T(8,128)} %convert_bitcast_fusion.gates_hbm, bf16[8,512,384]{2,1,0:T(8,128)(2,1)} %bitcast.6, bf16[8,512,384]{2,1,0:T(8,128)(2,1)} %bitcast.7, bf16[256,384]{1,0:T(8,128)(2,1)} %bitcast.8), custom_call_target="tpu_custom_call" | custom-call | flops 3221225472 | bytes 6291456 | tf_op jit(solution)/shard_map/pallas_call | solution.py:314
  42.3 1.5 %copy.8 = bf16[32,1024]{1,0:T(8,128)(2,1)} copy(bf16[32,1024]{1,0:T(8,128)(2,1)} %shard_map.64) | data formatting | bytes 131072

commit v3 on v2

--- a/solution.py
+++ b/solution.py
@@ -68,8 +68,8 @@
 
 
 def dense_kernel(
-    tok_hbm, routes_hbm, gates_hbm, wg_hbm, wu_hbm, hid_hbm, out_ref,
-    rt, gt, hid, w, x, gate_all, pre, grads, p_sib, r_sib, p_own, stage, recv, c_send, c_recv,
+    tok_hbm, routes_hbm, gt, wg_hbm, wu_hbm, hid_hbm, out_ref,
+    rt, hid, w, x, gate_all, pre, grads, p_sib, r_sib, p_own, stage, recv, c_send, c_recv,
     local_sem, send_sem, recv_sem,
 ):
     n_exp = 4
@@ -111,12 +111,11 @@
         pltpu.make_async_copy(tok_hbm.at[:, pl.ds(0, half)], x.at[2 * q, mine, :], local_sem.at[0]),
         pltpu.make_async_copy(tok_hbm.at[:, pl.ds(half, half)], x.at[2 * q + 1, mine, :], local_sem.at[1]),
         pltpu.make_async_copy(routes_hbm, rt, local_sem.at[2]),
-        pltpu.make_async_copy(gates_hbm, gt, local_sem.at[3]),
-        pltpu.make_async_copy(wg_hbm, w.at[:, :, pl.ds(0, ht)], local_sem.at[4]),
-        pltpu.make_async_copy(wu_hbm, w.at[:, :, pl.ds(ht, ht)], local_sem.at[5]),
-        pltpu.make_async_copy(hid_hbm, hid, local_sem.at[6]),
+        pltpu.make_async_copy(wg_hbm, w.at[:, :, pl.ds(0, ht)], local_sem.at[3]),
+        pltpu.make_async_copy(wu_hbm, w.at[:, :, pl.ds(ht, ht)], local_sem.at[4]),
+        pltpu.make_async_copy(hid_hbm, hid, local_sem.at[5]),
     ]
-    for c in loc[:4]:
+    for c in loc[:3]:
         c.start()
     barrier = pltpu.get_barrier_semaphore()
     partners = [to_x, to_y, to_c] + to_z[1:]
@@ -155,14 +154,13 @@
         core_copies[2][k] = same(block(qy, gx, zk[k]), to_c)
 
     column(0)
-    for c in loc[4:]:
+    for c in loc[3:]:
         c.start()
     loc[2].wait()
-    loc[3].wait()
     lanes = lax.broadcasted_iota(jnp.int32, (rows, 128), 1).astype(jnp.float32)
     table = jnp.zeros((rows, 128), jnp.float32)
     chosen = rt[...].astype(jnp.float32)
-    values = gt[...]
+    values = gt[...].astype(jnp.float32)
     shape = (rows, rows)
     eye = lax.broadcasted_iota(jnp.int32, shape, 0) == lax.broadcasted_iota(jnp.int32, shape, 1)
 
@@ -175,8 +173,8 @@
     gate_all[mine, :] = table.astype(jnp.bfloat16)
     own_gates = gate_all.at[mine, :]
     gz = [same(own_gates, to_z[k]) for k in (1, 2, 3)]
+    onward(0)
     column(1)
-    onward(0)
     column(2)
     onward(1)
     column(3)
@@ -186,7 +184,7 @@
     gcol = same(gate_column, to_x)
     onward(2)
     onward(3)
-    for c in loc[4:]:
+    for c in loc[3:]:
         c.wait()
 
     def first(quarter):
@@ -230,8 +228,8 @@
     for j in range(4):
         p_sib[j] = second(2 * (qcy if j < 2 else qc) + j % 2).astype(jnp.bfloat16)
         sib.append(remote(p_sib.at[j], r_sib.at[j], to_c))
-    for j in range(4):
-        p_own[j] = second(2 * (qy if j < 2 else q) + j % 2)
+    for j in (0, 1):
+        p_own[j] = second(2 * qy + j)
     da, db, sx, sy = {}, {}, {}, {}
 
     def own(j, gr, k):
@@ -277,6 +275,8 @@
     sib[1].wait_recv()
     diagonal(2)
     diagonal(3)
+    for j in (2, 3):
+        p_own[j] = second(2 * q + j % 2)
     sib[2].wait_recv()
     sib[3].wait_recv()
     plain(2)
@@ -314,11 +314,10 @@
     return pl.pallas_call(
         dense_kernel,
         out_shape=jax.ShapeDtypeStruct((rows, width), bf16),
-        in_specs=[any_space] * 6,
+        in_specs=[any_space] * 2 + [pl.BlockSpec(memory_space=pltpu.VMEM)] + [any_space] * 3,
         out_specs=pl.BlockSpec(memory_space=pltpu.VMEM),
         scratch_shapes=[
             pltpu.VMEM(routes.shape[::-1], jnp.int32),
-            pltpu.VMEM(gates.shape[::-1], f32),
             pltpu.VMEM((slots, ht), bf16),
             pltpu.VMEM((parts, half, 2 * ht), bf16),
             pltpu.VMEM((parts, slots, half), bf16),
@@ -332,7 +331,7 @@
             pltpu.VMEM((6, 4, rows, half), bf16),
             pltpu.VMEM((3, 2, rows, half), bf16),
             pltpu.VMEM((3, 2, rows, half), bf16),
-            pltpu.SemaphoreType.DMA((7,)),
+            pltpu.SemaphoreType.DMA((6,)),
             pltpu.SemaphoreType.DMA((n_copies,)),
             pltpu.SemaphoreType.DMA((n_copies,)),
         ],
@@ -345,7 +344,7 @@
     )(
         tokens,
         routes.T,
-        gates.T.astype(f32),
+        gates.T,
         w_gate.reshape(parts, half, ht),
         w_up.reshape(parts, half, ht),
         hidden_grad.reshape(slots, ht),

time: 44 us -> 43 us (0.977)
  other arithmetic: 1.27 us -> 0 us
    convert_element_type x1 -> x0, other arithmetic: 1.27 us -> none  [dense(): gates.T.astype(f32)]
where the time goes in v3:
time: 43 us; the launch traced here: 42.8 us
  Pallas kernels  41.3 us (96%)
  local copies, waits for them, and re-layouts  1.47 us (3%)
    pallas_call x1, Pallas kernels, dense(): pl.pallas_call(dense_kernel, out_shape=jax.ShapeDtypeStruct((rows, width)...  41.3 us
    unnamed x1, local copies, waits for them, and re-layouts  1.47 us

profile of v3, /device:TPU:0, one launch (start us, length us, event | category | flops | bytes accessed | tf_op | source)
XLA Modules:
  0.0 42.8 jit_solution(17887395583707107084)
XLA Ops:
  0.0 41.3 %shard_map.64 = bf16[32,1024]{1,0:T(8,128)(2,1)} custom-call(bf16[32,1024]{1,0:T(8,128)(2,1)} %tok_hbm.1, s32[8,32]{1,0:T(8,128)} %bitcast.8, bf16[8,32]{1,0:T(8,128)(2,1)} %bitcast.9, bf16[8,512,384]{2,1,0:T(8,128)(2,1)} %bitcast.5, bf16[8,512,384]{2,1,0:T(8,128)(2,1)} %bitcast.6, bf16[256,384]{1,0:T(8,128)(2,1)} %bitcast.7), custom_call_target="tpu_custom_call" | custom-call | flops 3221225472 | bytes 6291456 | tf_op jit(solution)/shard_map/pallas_call | solution.py:314
  41.3 1.5 %copy.8 = bf16[32,1024]{1,0:T(8,128)(2,1)} copy(bf16[32,1024]{1,0:T(8,128)(2,1)} %shard_map.64) | data formatting | bytes 131072

commit v4 on v3

--- a/solution.py
+++ b/solution.py
@@ -275,14 +275,14 @@
     sib[1].wait_recv()
     diagonal(2)
     diagonal(3)
+    diagonal(1)
+    diagonal(0)
     for j in (2, 3):
         p_own[j] = second(2 * q + j % 2)
     sib[2].wait_recv()
     sib[3].wait_recv()
     plain(2)
     plain(3)
-    diagonal(1)
-    diagonal(0)
     joined(2)
     joined(3)
     plain(1)

time: 43 us -> 43 us (level)
  no operation moved by 1% of the time
where the time goes in v4:
time: 43 us; the launch traced here: 42.8 us
  Pallas kernels  41.3 us (96%)
  local copies, waits for them, and re-layouts  1.47 us (3%)
    pallas_call x1, Pallas kernels, dense(): pl.pallas_call(dense_kernel, out_shape=jax.ShapeDtypeStruct((rows, width)...  41.3 us
    unnamed x1, local copies, waits for them, and re-layouts  1.47 us

profile of v4, /device:TPU:0, one launch (start us, length us, event | category | flops | bytes accessed | tf_op | source)
XLA Modules:
  0.0 42.8 jit_solution(14963408093327831172)
XLA Ops:
  0.0 41.3 %shard_map.64 = bf16[32,1024]{1,0:T(8,128)(2,1)} custom-call(bf16[32,1024]{1,0:T(8,128)(2,1)} %tok_hbm.1, s32[8,32]{1,0:T(8,128)} %bitcast.8, bf16[8,32]{1,0:T(8,128)(2,1)} %bitcast.9, bf16[8,512,384]{2,1,0:T(8,128)(2,1)} %bitcast.5, bf16[8,512,384]{2,1,0:T(8,128)(2,1)} %bitcast.6, bf16[256,384]{1,0:T(8,128)(2,1)} %bitcast.7), custom_call_target="tpu_custom_call" | custom-call | flops 3221225472 | bytes 6291456 | tf_op jit(solution)/shard_map/pallas_call | solution.py:314
  41.3 1.5 %copy.8 = bf16[32,1024]{1,0:T(8,128)(2,1)} copy(bf16[32,1024]{1,0:T(8,128)(2,1)} %shard_map.64) | data formatting | bytes 131072
